TPU v7x, 32 devices: a whole 2x2x4 slice. The times are simulated.
32 devices in a mesh: prow: 4 (over z), pcol: 4 (over y, core), skc: 2 (over x).
Axes of the slice: x: 2, y: 2, z: 4, core: 2. Of those that a mesh axis runs over, the one named last changes fastest.
Arguments:
- omega: float32 [256, 3, 16, 512], P('skc', None, 'prow', 'pcol'), may hold values from -4.1 to 4.1
- elastic: float32 [16, 512], P('prow', 'pcol'), may hold values from 0.25 to 3
- prony: float32 [4, 16, 512], P(None, 'prow', 'pcol'), may hold values from 0.1 to 1
- prony_weight: float32 [4], replicated, may hold values from 0.05 to 0.5
- coupling: float32 [9, 3, 3], replicated, may hold values from -0.03 to 0.03
Outputs:
- basis: float32 [256, 3, 16, 512], P('skc', None, 'prow', 'pcol')
- factor: float32 [256, 256], replicated
- gram: float32 [256, 256], replicated
All inputs are finite; a program needn't handle non-finite values.
Results may differ from a plain program's by a relative error of at most 0.001.
Values sent between devices are 32-bit elements; how exact they have to be, the bound alone decides.
A program may use at most 64 MiB of HBM per device.

v0:
```python
import functools
import math

import jax
import jax.numpy as jnp
from jax import lax
from jax.experimental import pallas as pl
from jax.experimental.pallas import tpu as pltpu
from jax.sharding import PartitionSpec as P

MESH = pl.DeviceIdType.MESH
HIGHEST = lax.Precision.HIGHEST
HALF = 128


def dot(a, b, dims, precision=HIGHEST):
    return lax.dot_general(
        a, b, (dims, ((), ())), precision=precision, preferred_element_type=jnp.float32
    )


NN = ((1,), (0,))
NT = ((1,), (1,))
TN = ((0,), (0,))


def reduce_kernel(planes, cols, rows, part_ref, out_ref, plane_buf, row_buf,
                  send_a, recv_a, send_b, recv_b, send_c, recv_c):
    me = lax.axis_index("pcol") * cols + lax.axis_index("skc")
    row = lax.axis_index("prow")
    chunk = part_ref.shape[0] // planes

    def at_plane(t):
        return {"pcol": t // cols, "skc": t % cols}

    def piece(ref, t):
        return ref.at[pl.ds(pl.multiple_of(t * chunk, 8), chunk)]

    others = [lax.rem(me + o, planes) for o in range(1, planes)]
    other_rows = [lax.rem(row + o, rows) for o in range(1, rows)]
    barrier = pltpu.get_barrier_semaphore()
    for t in others:
        pl.semaphore_signal(barrier, inc=1, device_id=at_plane(t), device_id_type=MESH)
    for t in other_rows:
        pl.semaphore_signal(barrier, inc=1, device_id={"prow": t}, device_id_type=MESH)
    pl.semaphore_wait(barrier, planes + rows - 2)

    def exchange(targets, where, source, target, mine, send, recv):
        sent = [
            pltpu.make_async_remote_copy(
                src_ref=source(t), dst_ref=target(mine), send_sem=send.at[t],
                recv_sem=recv.at[mine], device_id=where(t), device_id_type=MESH)
            for t in targets
        ]
        for copy in sent:
            copy.start()
        for t in targets:
            pltpu.make_async_remote_copy(
                src_ref=source(t), dst_ref=target(t), send_sem=send.at[t],
                recv_sem=recv.at[t], device_id=where(t), device_id_type=MESH).wait_recv()
        return sent

    sent = exchange(others, at_plane, lambda t: piece(part_ref, t), lambda t: plane_buf.at[t],
                    me, send_a, recv_a)
    plane_buf[me] = piece(part_ref, me)[...]
    total = plane_buf[0]
    for t in range(1, planes):
        total = total + plane_buf[t]
    row_buf[row] = total
    sent += exchange(other_rows, lambda t: {"prow": t}, lambda t: row_buf.at[row],
                     lambda t: row_buf.at[t], row, send_b, recv_b)
    total = row_buf[0]
    for t in range(1, rows):
        total = total + row_buf[t]
    piece(out_ref, me)[...] = total
    sent += exchange(others, at_plane, lambda t: piece(out_ref, me), lambda t: piece(out_ref, t),
                     me, send_c, recv_c)
    for copy in sent:
        copy.wait_send()


def reduce_all(part, name, collective_id):
    cols, rows = lax.axis_size("skc"), lax.axis_size("prow")
    planes = cols * lax.axis_size("pcol")
    chunk = part.shape[0] // planes
    dma = pltpu.SemaphoreType.DMA
    return pl.pallas_call(
        functools.partial(reduce_kernel, planes, cols, rows),
        out_shape=jax.ShapeDtypeStruct(part.shape, jnp.float32),
        in_specs=[pl.BlockSpec(memory_space=pltpu.VMEM)],
        out_specs=pl.BlockSpec(memory_space=pltpu.VMEM),
        scratch_shapes=[
            pltpu.VMEM((planes, chunk, part.shape[1]), jnp.float32),
            pltpu.VMEM((rows, chunk, part.shape[1]), jnp.float32),
            dma((planes,)), dma((planes,)), dma((rows,)), dma((rows,)),
            dma((planes,)), dma((planes,)),
        ],
        compiler_params=pltpu.CompilerParams(collective_id=collective_id, has_side_effects=True),
        name=name,
    )(part)


def eliminate(block):
    size = block.shape[0]
    tiles = size // 8
    lanes = lax.broadcasted_iota(jnp.int32, (8, size), 1)
    subs = lax.broadcasted_iota(jnp.int32, (8, size), 0)
    left = [block[8 * t : 8 * t + 8] for t in range(tiles)]
    right = [jnp.where(lanes == subs + 8 * t, 1.0, 0.0).astype(jnp.float32) for t in range(tiles)]

    def columns(tile, t):
        return [jnp.broadcast_to(tile[:, 8 * t + c : 8 * t + c + 1], (8, size)) for c in range(8)]

    def row(tile, s):
        return jnp.broadcast_to(tile[s : s + 1], (8, size))

    scales = []
    for t in range(tiles):
        cols = columns(left[t], t)
        inverses, pivots, rows_l, rows_r = [], [], [], []
        scale = None
        for s in range(8):
            pivot = row(cols[s], s)
            inverse = 1.0 / pivot
            scale = pivot if scale is None else jnp.where(subs == s, pivot, scale)
            rows_l.append(row(left[t], s))
            rows_r.append(row(right[t], s))
            inverses.append(inverse)
            if s == 7:
                pivots.append([])
                break
            factor = jnp.where(subs > s, cols[s] * inverse, 0.0)
            heads = [row(cols[c], s) for c in range(s + 1, 8)]
            pivots.append(heads)
            for c in range(s + 1, 8):
                cols[c] = cols[c] - factor * heads[c - s - 1]
            left[t] = left[t] - factor * rows_l[s]
            right[t] = right[t] - factor * rows_r[s]
        scales.append(lax.rsqrt(scale))
        for v in range(t + 1, tiles):
            cols = columns(left[v], t)
            for s in range(8):
                factor = cols[s] * inverses[s]
                for c in range(s + 1, 8):
                    cols[c] = cols[c] - factor * pivots[s][c - s - 1]
                left[v] = left[v] - factor * rows_l[s]
                right[v] = right[v] - factor * rows_r[s]
    upper = [jnp.where(lanes >= subs + 8 * t, left[t] * scales[t], 0.0) for t in range(tiles)]
    lower = [right[t] * scales[t] for t in range(tiles)]
    return jnp.concatenate(upper, axis=0), jnp.concatenate(lower, axis=0)


def factorize(gram_ref):
    h = HALF
    r11, i11 = eliminate(gram_ref[0:h])
    r12 = dot(i11, gram_ref[h : 2 * h], NN)
    r22, i22 = eliminate(gram_ref[2 * h : 3 * h] - dot(r12, r12, TN))
    i21 = -dot(i22, dot(r12, i11, TN), NN)
    zero = jnp.zeros((h, h), jnp.float32)
    upper = jnp.concatenate(
        [jnp.concatenate([r11, r12], axis=1), jnp.concatenate([zero, r22], axis=1)], axis=0)
    lower = jnp.concatenate(
        [jnp.concatenate([i11, zero], axis=1), jnp.concatenate([i21, i22], axis=1)], axis=0)
    return upper, lower


def sketch_kernel(cols, rows, planes, field_ref, modulus_ref, coupling_ref,
                  matrix_ref, part_ref, once, above, below, edges, arrived, halo,
                  send_row, recv_row, send_col, recv_col, send_skc, recv_skc):
    extent, comps, count, width = field_ref.shape
    blocks = extent * comps
    mine = lax.axis_index("skc")
    row, col = lax.axis_index("prow"), lax.axis_index("pcol")
    has = {-1: row > 0, 0: None, 1: row < rows - 1}
    has_col = {-1: col > 0, 1: col < planes - 1}
    corners = [(a, b) for b in (-1, 1) for a in (-1, 0, 1)]

    def exists(a, b):
        if b == 0:
            return has[a]
        return has_col[b] if a == 0 else jnp.logical_and(has[a], has_col[b])

    def at(a, b):
        return {"prow": row + a, "pcol": col + b}

    def skc_peer(o):
        return lax.rem(mine + o, cols)

    directions = corners + [(-1, 0), (1, 0)]
    above[...] = jnp.zeros_like(above)
    below[...] = jnp.zeros_like(below)
    arrived[...] = jnp.zeros_like(arrived)
    barrier = pltpu.get_barrier_semaphore()
    for a, b in directions:
        @pl.when(exists(a, b))
        def _():
            pl.semaphore_signal(barrier, inc=1, device_id=at(a, b), device_id_type=MESH)
    for o in range(1, cols):
        pl.semaphore_signal(barrier, inc=1, device_id={"skc": skc_peer(o)}, device_id_type=MESH)
    ends = [jnp.where(row > 0, 1, 0) + jnp.where(row < rows - 1, 1, 0),
            jnp.where(col > 0, 1, 0) + jnp.where(col < planes - 1, 1, 0)]
    pl.semaphore_wait(barrier, (ends[0] + 1) * (ends[1] + 1) - 1 + cols - 1)

    lanes = lax.broadcasted_iota(jnp.int32, (8, width), 1)
    wide = lax.broadcasted_iota(jnp.int32, (count, width), 1)

    def row_copy(source, step, a):
        index = 2 * step + (0 if a < 0 else 1)
        target = below if a < 0 else above
        return pltpu.make_async_remote_copy(
            src_ref=source.at[0 if a < 0 else extent - 1], dst_ref=target.at[step],
            send_sem=send_row.at[index], recv_sem=recv_row.at[index],
            device_id=at(a, 0), device_id_type=MESH)

    def col_copy(step, a, b):
        index = 6 * step + corners.index((a, b))
        return pltpu.make_async_remote_copy(
            src_ref=edges.at[2 * step + (0 if b < 0 else 1)], dst_ref=arrived.at[index],
            send_sem=send_col.at[index], recv_sem=recv_col.at[index],
            device_id=at(a, b), device_id_type=MESH)

    def exchange(source, step):
        for a in (-1, 1):
            @pl.when(exists(a, 0))
            def _():
                row_copy(source, step, a).start()
        for b in (-1, 1):
            packed = jnp.zeros((count, width), jnp.float32)
            for p in range(blocks):
                place = source[p // comps, p % comps]
                edge = place[:, 0:1] if b < 0 else place[:, width - 1 : width]
                packed = jnp.where(wide == p, edge, packed)
            edges[2 * step + (0 if b < 0 else 1)] = packed.T[: edges.shape[1]]
        for a, b in corners:
            @pl.when(exists(a, b))
            def _():
                col_copy(step, a, b).start()
        for a, b in corners:
            @pl.when(exists(-a, -b))
            def _():
                col_copy(step, a, b).wait_recv()
        pad = jnp.zeros((width - blocks - 2 * comps, count), jnp.float32)
        for b in (-1, 1):
            index = 6 * step
            centre = arrived[index + corners.index((0, b))][:blocks]
            upper = arrived[index + corners.index((1, b))][blocks - comps : blocks]
            under = arrived[index + corners.index((-1, b))][:comps]
            halo[0 if b > 0 else 1] = jnp.concatenate([upper, centre, under, pad], axis=0).T
        for a in (-1, 1):
            @pl.when(exists(-a, 0))
            def _():
                row_copy(source, step, a).wait_recv()

    def apply(source, step, store):
        def tile(k, carry):
            at_k = pl.ds(pl.multiple_of(k * 8, 8), 8)
            acc = [[source[x, i, at_k] for x in range(extent)] for i in range(comps)]
            before, after = halo[0, at_k], halo[1, at_k]
            for j in range(comps):
                plain = [above[step, j, at_k]] + [source[x, j, at_k] for x in range(extent)]
                plain.append(below[step, j, at_k])
                for c in range(3):
                    if c == 1:
                        shifted = plain
                    else:
                        edge, hide, turn = (before, 0, 1) if c == 0 else (after, width - 1, width - 1)
                        shifted = [
                            jnp.where(lanes == hide, edge[:, comps * x + j : comps * x + j + 1],
                                      pltpu.roll(plain[x], turn, 1))
                            for x in range(extent + 2)
                        ]
                    for r in range(3):
                        for i in range(comps):
                            weight = coupling_ref[(3 * r + c) * comps * comps + i * comps + j]
                            for x in range(extent):
                                acc[i][x] = acc[i][x] + weight * shifted[x + r]
            for i in range(comps):
                for x in range(extent):
                    store(x, i, k, modulus_ref[x : x + 1, :] * acc[i][x])
            return carry

        lax.fori_loop(0, count // 8, tile, 0)

    def store_once(x, i, k, value):
        once[x, i, pl.ds(pl.multiple_of(k * 8, 8), 8)] = value

    def store_last(x, i, k, value):
        start = pl.multiple_of(mine * count + k * 8, 8)
        matrix_ref[comps * x + i, pl.ds(start, 8)] = value

    exchange(field_ref, 0)
    apply(field_ref, 0, store_once)
    exchange(once, 1)
    apply(once, 1, store_last)

    share = blocks // cols

    def skc_copy(owner, to, part, o):
        place = matrix_ref.at[pl.ds(part * share, share), pl.ds(pl.multiple_of(owner * count, 8), count)]
        return pltpu.make_async_remote_copy(
            src_ref=place, dst_ref=place, send_sem=send_skc.at[o], recv_sem=recv_skc.at[o],
            device_id={"skc": to}, device_id_type=MESH)

    pairs = [(q, o) for q in range(cols) for o in range(1, cols)]
    for n, (q, o) in enumerate(pairs):
        to = skc_peer(o)
        skc_copy(mine, to, lax.rem(to + q, cols), n).start()
    for n, (q, o) in enumerate(pairs[: cols - 1]):
        owner = lax.rem(mine + cols - o, cols)
        skc_copy(owner, owner, mine, n).wait_recv()
    part_ref[...] = pack_blocks(matrix_ref, mine * share, share)
    for n, (q, o) in enumerate(pairs):
        if q > 0:
            owner = lax.rem(mine + cols - o, cols)
            skc_copy(owner, owner, lax.rem(mine + q, cols), n).wait_recv()
    for n, (q, o) in enumerate(pairs):
        to = skc_peer(o)
        skc_copy(mine, to, lax.rem(to + q, cols), n).wait_send()
    for step in range(2):
        source = field_ref if step == 0 else once
        for a in (-1, 1):
            @pl.when(exists(a, 0))
            def _():
                row_copy(source, step, a).wait_send()
        for a, b in corners:
            @pl.when(exists(a, b))
            def _():
                col_copy(step, a, b).wait_send()


def pack_blocks(ref, start, share):
    total = None
    for p in range(share):
        block = ref[start + p]
        first, second = block[:HALF], block[HALF:]
        terms = [dot(first, first, NT), dot(first, second, NT), dot(second, second, NT)]
        total = terms if total is None else [s + t for s, t in zip(total, terms)]
    return jnp.concatenate(total, axis=0)


def sketch(field, modulus, coupling):
    extent, comps, count, width = field.shape
    cols, rows, planes = (lax.axis_size(a) for a in ("skc", "prow", "pcol"))
    blocks = extent * comps
    edge_rows = -(-blocks // 8) * 8
    dma = pltpu.SemaphoreType.DMA
    vmem = pl.BlockSpec(memory_space=pltpu.VMEM)
    f32 = jnp.float32
    return pl.pallas_call(
        functools.partial(sketch_kernel, cols, rows, planes),
        out_shape=[
            jax.ShapeDtypeStruct((blocks, count * cols, width), f32),
            jax.ShapeDtypeStruct((3 * HALF, HALF), f32),
        ],
        in_specs=[vmem, vmem, pl.BlockSpec(memory_space=pltpu.SMEM)],
        out_specs=[vmem, vmem],
        scratch_shapes=[
            pltpu.VMEM((extent, comps, count, width), f32),
            pltpu.VMEM((2, comps, count, width), f32),
            pltpu.VMEM((2, comps, count, width), f32),
            pltpu.VMEM((4, edge_rows, count), f32),
            pltpu.VMEM((12, edge_rows, count), f32),
            pltpu.VMEM((2, count, width), f32),
            dma((4,)), dma((4,)), dma((12,)), dma((12,)),
            dma((cols * (cols - 1),)), dma((cols * (cols - 1),)),
        ],
        compiler_params=pltpu.CompilerParams(
            collective_id=3, has_side_effects=True, vmem_limit_bytes=40 * 1024 * 1024),
        name="sketch",
    )(field, modulus, coupling)


def first_kernel(groups, gram_ref, matrix_ref, upper_ref, ortho_ref, part_ref):
    upper, lower = factorize(gram_ref)
    upper_ref[...] = upper
    blocks = matrix_ref.shape[0]
    for p in range(blocks):
        ortho_ref[p] = dot(lower, matrix_ref[p], NN)
    share = blocks // groups
    part_ref[...] = pack_blocks(ortho_ref, lax.axis_index("skc") * share, share)


def second_kernel(scale, groups, gram_ref, upper_ref, ortho_ref, out_ref, factor_ref, lower_ref):
    upper, lower = factorize(gram_ref)
    factor_ref[...] = dot(upper, upper_ref[...], NN) * (1.0 / scale)
    count = lower.shape[0] // groups
    lower_ref[...] = lower * scale
    own = lower_ref[pl.ds(pl.multiple_of(lax.axis_index("skc") * count, 8), count)]
    for p in range(ortho_ref.shape[0]):
        out_ref[p] = dot(own, ortho_ref[p], NN)


def call(kernel, outs, name, scratch=()):
    return pl.pallas_call(
        kernel,
        out_shape=[jax.ShapeDtypeStruct(s, jnp.float32) for s in outs],
        scratch_shapes=[pltpu.VMEM(s, jnp.float32) for s in scratch],
        compiler_params=pltpu.CompilerParams(vmem_limit_bytes=40 * 1024 * 1024),
        name=name,
    )


def body(omega, elastic, prony, prony_weight, coupling):
    modulus = elastic + jnp.sum(prony_weight[:, None, None] * prony, axis=0)
    local_cols, comps, extent_x, extent_y = omega.shape
    groups = lax.axis_size("skc")
    total_cols = local_cols * groups
    blocks = comps * extent_x
    row_count = blocks * extent_y * lax.axis_size("prow") * lax.axis_size("pcol")
    root_rows = math.sqrt(row_count)
    matrix, part_one = sketch(omega.transpose(2, 1, 0, 3), modulus, coupling.reshape(-1))
    gram_one = reduce_all(part_one, "sum_first", 1)
    square = (total_cols, total_cols)
    upper_one, ortho_once, part_two = call(
        functools.partial(first_kernel, groups),
        [square, matrix.shape, (3 * HALF, HALF)], "first")(gram_one, matrix)
    gram_two = reduce_all(part_two, "sum_second", 2)
    own_rows, factor = call(
        functools.partial(second_kernel, root_rows, groups),
        [(blocks, local_cols, extent_y), square], "second", [square])(
            gram_two, upper_one, ortho_once)
    basis = own_rows.reshape(extent_x, comps, local_cols, extent_y).transpose(2, 1, 0, 3)
    aa, ab, bb = gram_one[:HALF], gram_one[HALF : 2 * HALF], gram_one[2 * HALF :]
    gram = jnp.concatenate(
        [jnp.concatenate([aa, ab], axis=1), jnp.concatenate([ab.T, bb], axis=1)], axis=0)
    return (basis, factor, gram / row_count)


def solution(mesh):
    in_specs = (
        P("skc", None, "prow", "pcol"),
        P("prow", "pcol"),
        P(None, "prow", "pcol"),
        P(),
        P(),
    )
    out_specs = (P("skc", None, "prow", "pcol"), P(), P())
    return jax.shard_map(body, mesh=mesh, in_specs=in_specs, out_specs=out_specs, check_vma=False)
```

profile of v0, /device:TPU:0, one launch (start us, length us, event | category | flops | bytes accessed | tf_op | source)
XLA Modules:
  0.0 109.7 jit_solution(4867231282519277659)
XLA Ops:
  0.6 0.0 copy-start.9
  0.6 0.0 copy-start.7
  0.7 0.0 copy-start.10
  0.7 0.0 copy-start.8
  0.7 1.2 %copy.19 = f32[128,3,4,128]{3,0,1,2:T(8,128)S(1)} copy(f32[128,3,4,128]{3,2,1,0:T(4,128)} %param.5) | data formatting | bytes 1572864 | tf_op args[0]
  1.9 0.0 copy-done.7
  1.9 0.0 copy-done.10
  1.9 0.1 multiply_reduce_fusion
  2.0 0.0 copy-done.9
  2.0 0.0 copy-done.8
  2.0 0.1 copy.13
  2.1 0.1 reshape.13.coupling_ref
  2.2 43.7 %sketch.1 = (f32[12,256,128]{2,1,0:T(8,128)S(1)}, f32[384,128]{1,0:T(8,128)S(1)}) custom-call(f32[4,3,128,128]{3,2,1,0:T(8,128)S(1)} %bitcast.9, f32[4,128]{1,0:T(4,128)S(1)} %add.3.modulus_ref, f32[81]{0:T(128)S(1)} %reshape.13.coupling_ref), custom_call_target="tpu_custom_call" | custom-call | tf_op jit(solution)/shard_map/sketch/pallas_call | solution.py:349
  45.9 0.0 copy-start.5
  45.9 0.7 copy-done.5
  46.6 15.2 %sum_first.1.gram_ref = f32[384,128]{1,0:T(8,128)} custom-call(f32[384,128]{1,0:T(8,128)} %copy-done.5), custom_call_target="tpu_custom_call" | custom-call | tf_op jit(solution)/shard_map/sum_first/pallas_call | solution.py:87
  61.8 0.0 copy-start
  61.8 0.9 copy-done
  62.7 14.1 %first.1 = (f32[256,256]{1,0:T(8,128)S(1)}, f32[12,256,128]{2,1,0:T(8,128)S(1)}, f32[384,128]{1,0:T(8,128)S(1)}) custom-call(f32[384,128]{1,0:T(8,128)S(1)} %copy-done, f32[12,256,128]{2,1,0:T(8,128)S(1)} %get-tuple-element.11.matrix_ref), custom_call_target="tpu_custom_call" | custom-call | tf_op jit(solution)/shard_map/first/pallas_call | solution.py:414
  76.8 0.0 copy-start.2
  76.8 1.2 %copy-done.2 = f32[12,256,128]{2,1,0:T(8,128)} copy-done((f32[12,256,128]{2,1,0:T(8,128)}, f32[12,256,128]{2,1,0:T(8,128)S(1)}, u32[]{:S(2)}) %copy-start.2) | copy-done | bytes 1572888
  78.0 0.0 copy-start.6
  78.0 0.7 copy-done.6
  78.6 15.8 %sum_second.1.gram_ref = f32[384,128]{1,0:T(8,128)} custom-call(f32[384,128]{1,0:T(8,128)} %copy-done.6), custom_call_target="tpu_custom_call" | custom-call | tf_op jit(solution)/shard_map/sum_second/pallas_call | solution.py:87
  94.5 0.0 copy-start.3
  94.5 1.4 %copy-done.3 = f32[12,256,128]{2,1,0:T(8,128)S(1)} copy-done((f32[12,256,128]{2,1,0:T(8,128)S(1)}, f32[12,256,128]{2,1,0:T(8,128)}, u32[]{:S(2)}) %copy-start.3) | copy-done | bytes 1572888
  95.9 0.9 copy-done.4
  96.8 10.6 %second.1 = (f32[12,128,128]{2,1,0:T(8,128)S(1)}, f32[256,256]{1,0:T(8,128)}) custom-call(f32[384,128]{1,0:T(8,128)S(1)} %copy-done.4, f32[256,256]{1,0:T(8,128)S(1)} %get-tuple-element.13.upper_ref, f32[12,256,128]{2,1,0:T(8,128)S(1)} %copy-done.3), custom_call_target="tpu_custom_call" | custom-call | tf_op jit(solution)/shard_map/second/pallas_call | solution.py:418
  107.4 1.4 %copy.18 = f32[4,3,128,128]{3,0,1,2:T(4,128)} copy(f32[4,3,128,128]{3,2,1,0:T(8,128)S(1)} %bitcast.10) | data formatting | bytes 1572864 | tf_op jit(solution)/shard_map/reshape | solution.py:422
  108.8 0.0 copy-done.1
  108.8 0.1 copy.15
  108.9 0.7 maximum_multiply_fusion
  (4 shorter events, 0.0 us)
Async XLA Ops:
  0.6 1.4 %copy-start.9 = (f32[4,128]{1,0:T(4,128)S(1)}, f32[4,128]{1,0:T(4,128)}, u32[]{:S(2)}) copy-start(f32[4,128]{1,0:T(4,128)} %param.6) | copy-start | bytes 6148
  0.6 1.2 %copy-start.7 = (f32[4,4,128]{2,1,0:T(4,128)S(1)}, f32[4,4,128]{2,1,0:T(4,128)}, u32[]{:S(2)}) copy-start(f32[4,4,128]{2,1,0:T(4,128)} %param.7) | copy-start | bytes 24580
  0.7 1.2 %copy-start.10 = (f32[4]{0:T(128)S(1)}, f32[4]{0:T(128)}, u32[]{:S(2)}) copy-start(f32[4]{0:T(128)} %param.8) | copy-start | bytes 52
  0.7 1.3 %copy-start.8 = (f32[9,3,3]{0,2,1:T(4,128)S(1)}, f32[9,3,3]{0,2,1:T(4,128)}, u32[]{:S(2)}) copy-start(f32[9,3,3]{0,2,1:T(4,128)} %param.9) | copy-start | bytes 976
  45.9 0.7 copy-start.5
  61.8 0.9 copy-start
  76.8 1.2 %copy-start.2 = (f32[12,256,128]{2,1,0:T(8,128)}, f32[12,256,128]{2,1,0:T(8,128)S(1)}, u32[]{:S(2)}) copy-start(f32[12,256,128]{2,1,0:T(8,128)S(1)} %get-tuple-element.14.ortho_ref) | copy-start | bytes 4718596
  78.0 0.7 copy-start.6
  94.5 1.4 %copy-start.3 = (f32[12,256,128]{2,1,0:T(8,128)S(1)}, f32[12,256,128]{2,1,0:T(8,128)}, u32[]{:S(2)}) copy-start(f32[12,256,128]{2,1,0:T(8,128)} %copy-done.2) | copy-start | bytes 4718596
  95.9 0.9 copy-start.4
  96.8 12.0 %copy-start.1 = (f32[384,128]{1,0:T(8,128)S(1)}, f32[384,128]{1,0:T(8,128)}, u32[]{:S(2)}) copy-start(f32[384,128]{1,0:T(8,128)} %sum_first.1.gram_ref) | copy-start | bytes 589828
where the time goes:
time: 110 us
  Pallas kernels  99.4 us (90%)
  local copies, waits for them, and re-layouts  8.69 us (8%)
    pallas_call x1, Pallas kernels, sketch(): pl.pallas_call(functools.partial(sketch_kernel, cols, rows, planes), out_...  43.7 us
    pallas_call x2, Pallas kernels, reduce_all(): pl.pallas_call(functools.partial(reduce_kernel, planes, cols, rows), out_...  31 us
    pallas_call x1, Pallas kernels, body(): call(functools.partial(first_kernel, groups), [square, matrix.shape, (3 *...  14.1 us
    pallas_call x1, Pallas kernels, body(): call(functools.partial(second_kernel, root_rows, groups), [(blocks, local...  10.6 us
    unnamed x24, local copies, waits for them, and re-layouts  7.09 us

commit v1 on v0

--- a/solution.py
+++ b/solution.py
@@ -301,7 +301,7 @@
             src_ref=place, dst_ref=place, send_sem=send_skc.at[o], recv_sem=recv_skc.at[o],
             device_id={"skc": to}, device_id_type=MESH)
 
-    pairs = [(q, o) for q in range(cols) for o in range(1, cols)]
+    pairs = [(0, o) for o in range(1, cols)]
     for n, (q, o) in enumerate(pairs):
         to = skc_peer(o)
         skc_copy(mine, to, lax.rem(to + q, cols), n).start()
@@ -309,10 +309,6 @@
         owner = lax.rem(mine + cols - o, cols)
         skc_copy(owner, owner, mine, n).wait_recv()
     part_ref[...] = pack_blocks(matrix_ref, mine * share, share)
-    for n, (q, o) in enumerate(pairs):
-        if q > 0:
-            owner = lax.rem(mine + cols - o, cols)
-            skc_copy(owner, owner, lax.rem(mine + q, cols), n).wait_recv()
     for n, (q, o) in enumerate(pairs):
         to = skc_peer(o)
         skc_copy(mine, to, lax.rem(to + q, cols), n).wait_send()
@@ -362,7 +358,7 @@
             pltpu.VMEM((12, edge_rows, count), f32),
             pltpu.VMEM((2, count, width), f32),
             dma((4,)), dma((4,)), dma((12,)), dma((12,)),
-            dma((cols * (cols - 1),)), dma((cols * (cols - 1),)),
+            dma((cols - 1,)), dma((cols - 1,)),
         ],
         compiler_params=pltpu.CompilerParams(
             collective_id=3, has_side_effects=True, vmem_limit_bytes=40 * 1024 * 1024),
@@ -370,24 +366,41 @@
     )(field, modulus, coupling)
 
 
-def first_kernel(groups, gram_ref, matrix_ref, upper_ref, ortho_ref, part_ref):
+def first_kernel(groups, gram_ref, matrix_ref, upper_ref, lower_ref, ortho_ref, part_ref):
     upper, lower = factorize(gram_ref)
     upper_ref[...] = upper
-    blocks = matrix_ref.shape[0]
-    for p in range(blocks):
-        ortho_ref[p] = dot(lower, matrix_ref[p], NN)
-    share = blocks // groups
-    part_ref[...] = pack_blocks(ortho_ref, lax.axis_index("skc") * share, share)
-
-
-def second_kernel(scale, groups, gram_ref, upper_ref, ortho_ref, out_ref, factor_ref, lower_ref):
+    lower_ref[...] = lower
+    share = matrix_ref.shape[0] // groups
+    start = lax.axis_index("skc") * share
+    for p in range(share):
+        ortho_ref[p] = dot(lower, matrix_ref[start + p], NN)
+    part_ref[...] = pack_blocks(ortho_ref, 0, share)
+
+
+def second_kernel(scale, groups, gram_ref, upper_one_ref, lower_one_ref, ortho_ref, matrix_ref,
+                  *refs):
+    rest, (out_ref, factor_ref, lower_ref, block_ref) = refs[: groups - 1], refs[groups - 1 :]
     upper, lower = factorize(gram_ref)
-    factor_ref[...] = dot(upper, upper_ref[...], NN) * (1.0 / scale)
+    factor_ref[...] = dot(upper, upper_one_ref[...], NN) * (1.0 / scale)
     count = lower.shape[0] // groups
+    mine = lax.axis_index("skc")
+    share = ortho_ref.shape[0]
     lower_ref[...] = lower * scale
-    own = lower_ref[pl.ds(pl.multiple_of(lax.axis_index("skc") * count, 8), count)]
-    for p in range(ortho_ref.shape[0]):
-        out_ref[p] = dot(own, ortho_ref[p], NN)
+    place = pl.ds(pl.multiple_of(mine * count, 8), count)
+    own = lower_ref[place]
+    for p in range(share):
+        out_ref[mine * share + p] = dot(own, ortho_ref[p], NN)
+    both = dot(own, lower_one_ref[...], NN)
+    for q in range(1, groups):
+        start = lax.rem(mine + q, groups) * share
+        for p in range(share):
+            slot = (q - 1) * share + p
+            block_ref[slot, place] = matrix_ref[start + p, place]
+            for o in range(1, groups):
+                owner = lax.rem(mine + groups - o, groups)
+                there = pl.ds(pl.multiple_of(owner * count, 8), count)
+                block_ref[slot, there] = rest[o - 1][slot]
+            out_ref[start + p] = dot(both, block_ref[slot], NN)
 
 
 def call(kernel, outs, name, scratch=()):
@@ -396,8 +409,25 @@
         out_shape=[jax.ShapeDtypeStruct(s, jnp.float32) for s in outs],
         scratch_shapes=[pltpu.VMEM(s, jnp.float32) for s in scratch],
         compiler_params=pltpu.CompilerParams(vmem_limit_bytes=40 * 1024 * 1024),
+        cost_estimate=pl.CostEstimate(
+            flops=5 * 10**9, bytes_accessed=4 * 10**7, transcendentals=0),
         name=name,
     )
+
+
+def remaining(matrix, count, groups):
+    share = matrix.shape[0] // groups
+    mine = lax.axis_index("skc")
+    for offset in range(1, groups):
+        to = lax.rem(mine + offset, groups)
+        pieces = [
+            lax.dynamic_slice(
+                matrix, (lax.rem(to + q, groups) * share, mine * count, 0),
+                (share, count, matrix.shape[2]))
+            for q in range(1, groups)
+        ]
+        payload = pieces[0] if groups == 2 else jnp.concatenate(pieces, axis=0)
+        yield lax.ppermute(payload, "skc", [(i, (i + offset) % groups) for i in range(groups)])
 
 
 def body(omega, elastic, prony, prony_weight, coupling):
@@ -410,15 +440,20 @@
     root_rows = math.sqrt(row_count)
     matrix, part_one = sketch(omega.transpose(2, 1, 0, 3), modulus, coupling.reshape(-1))
     gram_one = reduce_all(part_one, "sum_first", 1)
+    gram_one, later = lax.optimization_barrier((gram_one, matrix))
+    rest = list(remaining(later, local_cols, groups))
     square = (total_cols, total_cols)
-    upper_one, ortho_once, part_two = call(
+    share = blocks // groups
+    upper_one, lower_one, ortho_once, part_two = call(
         functools.partial(first_kernel, groups),
-        [square, matrix.shape, (3 * HALF, HALF)], "first")(gram_one, matrix)
+        [square, square, (share, total_cols, extent_y), (3 * HALF, HALF)], "first")(
+            gram_one, matrix)
     gram_two = reduce_all(part_two, "sum_second", 2)
     own_rows, factor = call(
         functools.partial(second_kernel, root_rows, groups),
-        [(blocks, local_cols, extent_y), square], "second", [square])(
-            gram_two, upper_one, ortho_once)
+        [(blocks, local_cols, extent_y), square], "second",
+        [square, (blocks - share, total_cols, extent_y)])(
+            gram_two, upper_one, lower_one, ortho_once, matrix, *rest)
     basis = own_rows.reshape(extent_x, comps, local_cols, extent_y).transpose(2, 1, 0, 3)
     aa, ab, bb = gram_one[:HALF], gram_one[HALF : 2 * HALF], gram_one[2 * HALF :]
     gram = jnp.concatenate(

time: 110 us -> 104 us (0.945)
  Pallas kernels: 99.4 us -> 92.1 us
  starting transfers between devices: 0 us -> 1.27 us
    pallas_call x1, Pallas kernels: 43.7 us -> 37.8 us  [sketch(): pl.pallas_call(functools.partial(sketch_kernel, cols, rows, planes), out_...]
    pallas_call x1, Pallas kernels: 14.1 us -> 12.5 us  [body(): call(functools.partial(first_kernel, groups), [square, square, (share, to...]
    ppermute x0 -> x1, starting transfers between devices: none -> 1.27 us  [remaining(): lax.ppermute(payload, 'skc', [(i, (i + offset) % groups) for i in range(g...]
  transfers between devices with their start and end apart: 0 -> 1, of which waited for: 0 -> 0; matrix products, arithmetic and copies ran while one was open for 0% -> 1% of each run, Pallas kernels for 0% -> 27%
where the time goes in v1:
time: 104 us
  Pallas kernels  92.1 us (89%)
  local copies, waits for them, and re-layouts  8.57 us (8%)
  starting transfers between devices  1.27 us (1%)
    pallas_call x1, Pallas kernels, sketch(): pl.pallas_call(functools.partial(sketch_kernel, cols, rows, planes), out_...  37.8 us
    pallas_call x2, Pallas kernels, reduce_all(): pl.pallas_call(functools.partial(reduce_kernel, planes, cols, rows), out_...  30.7 us
    pallas_call x1, Pallas kernels, body(): call(functools.partial(first_kernel, groups), [square, square, (share, to...  12.5 us
    pallas_call x1, Pallas kernels, body(): call(functools.partial(second_kernel, root_rows, groups), [(blocks, local...  11.2 us
    unnamed x24, local copies, waits for them, and re-layouts  6.18 us
  transfers between devices with their start and end apart: 1, of which 0 were waited for; matrix products, arithmetic and copies ran while one was open for 1% of the time, Pallas kernels for 27%

profile of v1, /device:TPU:0, one launch (start us, length us, event | category | flops | bytes accessed | tf_op | source)
XLA Modules:
  0.0 103.6 jit_solution(9931396757753158167)
XLA Ops:
  0.6 0.0 copy-start.8
  0.6 0.0 copy-start.7
  0.7 0.0 copy-start.10
  0.7 0.0 copy-start.9
  0.7 1.2 %copy.19 = f32[128,3,4,128]{3,0,1,2:T(8,128)S(1)} copy(f32[128,3,4,128]{3,2,1,0:T(4,128)} %param.5) | data formatting | bytes 1572864 | tf_op args[0]
  1.9 0.0 copy-done.8
  1.9 0.1 copy.13
  2.0 0.1 reshape.13.coupling_ref
  2.1 0.0 copy-done.7
  2.1 0.0 copy-done.10
  2.1 0.1 multiply_reduce_fusion
  2.2 0.0 copy-done.9
  2.2 37.8 %sketch.1 = (f32[12,256,128]{2,1,0:T(8,128)S(1)}, f32[384,128]{1,0:T(8,128)S(1)}) custom-call(f32[4,3,128,128]{3,2,1,0:T(8,128)S(1)} %bitcast.9, f32[4,128]{1,0:T(4,128)S(1)} %add.15.modulus_ref, f32[81]{0:T(128)S(1)} %reshape.13.coupling_ref), custom_call_target="tpu_custom_call" | custom-call | tf_op jit(solution)/shard_map/sketch/pallas_call | solution.py:345
  40.0 0.0 copy-start.3
  40.0 0.7 copy-done.3
  40.7 15.2 %sum_first.1.gram_ref = f32[384,128]{1,0:T(8,128)} custom-call(f32[384,128]{1,0:T(8,128)} %copy-done.3), custom_call_target="tpu_custom_call" | custom-call | tf_op jit(solution)/shard_map/sum_first/pallas_call | solution.py:87
  55.9 0.8 constant_dynamic-slice_fusion
  56.6 1.3 %collective-permute-start = (f32[6,128,128]{2,1,0:T(8,128)}, f32[6,128,128]{2,1,0:T(8,128)S(1)}, u32[]{:S(2)}, u32[]{:S(2)}) collective-permute-start(f32[6,128,128]{2,1,0:T(8,128)} %constant_dynamic-slice_fusion), channel_id=1, source_target_pairs={{0,1},{1,0},{2,3},{3,2},{4,5},{5,4},{6,7},{7,6},{8,9},{9,8},{10,11... | collective-permute-start | bytes 1179656 | tf_op jit(solution)/shard_map/ppermute | solution.py:430
  57.9 0.9 copy-done
  58.8 12.5 %first.1 = (f32[256,256]{1,0:T(8,128)S(1)}, f32[256,256]{1,0:T(8,128)S(1)}, f32[6,256,128]{2,1,0:T(8,128)S(1)}, f32[384,128]{1,0:T(8,128)S(1)}) custom-call(f32[384,128]{1,0:T(8,128)S(1)} %copy-done, f32[12,256,128]{2,1,0:T(8,128)S(1)} %get-tuple-element.20.matrix_ref), custom_call_target="tpu_custom_call" | custom-call | flops 5000000000 | bytes 40000000 | tf_op jit(solution)/shard_map/first/pallas_call | solution.py:447
  71.4 0.0 copy-start.4
  71.4 0.7 copy-done.4
  72.0 0.7 copy-done.5
  72.7 15.5 %sum_second.1.gram_ref = f32[384,128]{1,0:T(8,128)} custom-call(f32[384,128]{1,0:T(8,128)} %copy-done.4), custom_call_target="tpu_custom_call" | custom-call | tf_op jit(solution)/shard_map/sum_second/pallas_call | solution.py:87
  88.2 0.0 copy-done.1
  88.3 0.1 copy.15
  88.4 0.7 maximum_multiply_fusion
  89.1 0.0 collective-permute-done.refs_0_
  89.1 0.9 copy-done.2
  90.0 0.9 copy-done.6
  91.0 11.2 %second.1 = (f32[12,128,128]{2,1,0:T(8,128)S(1)}, f32[256,256]{1,0:T(8,128)}) custom-call(f32[384,128]{1,0:T(8,128)S(1)} %copy-done.2, f32[256,256]{1,0:T(8,128)S(1)} %get-tuple-element.17.upper_one_ref, f32[256,256]{1,0:T(8,128)S(1)} %copy-done.6, f32[6,256,128]{2,1,0:T(8,128)S(1)} %get-tuple-element.19.ortho_ref, ...), custom_call_target="tpu_custom_call" | custom-call | flops 5000000000 | bytes 40000000 | tf_op jit(solution)/shard_map/second/pallas_call | solution.py:452
  102.2 1.4 %copy.18 = f32[4,3,128,128]{3,0,1,2:T(4,128)} copy(f32[4,3,128,128]{3,2,1,0:T(8,128)S(1)} %bitcast.10) | data formatting | bytes 1572864 | tf_op jit(solution)/shard_map/reshape | solution.py:457
  (7 shorter events, 0.0 us)
Async XLA Ops:
  0.6 1.3 %copy-start.8 = (f32[9,3,3]{0,2,1:T(4,128)S(1)}, f32[9,3,3]{0,2,1:T(4,128)}, u32[]{:S(2)}) copy-start(f32[9,3,3]{0,2,1:T(4,128)} %param.9) | copy-start | bytes 976
  0.6 1.5 %copy-start.7 = (f32[4,4,128]{2,1,0:T(4,128)S(1)}, f32[4,4,128]{2,1,0:T(4,128)}, u32[]{:S(2)}) copy-start(f32[4,4,128]{2,1,0:T(4,128)} %param.7) | copy-start | bytes 24580
  0.7 1.5 %copy-start.10 = (f32[4]{0:T(128)S(1)}, f32[4]{0:T(128)}, u32[]{:S(2)}) copy-start(f32[4]{0:T(128)} %param.8) | copy-start | bytes 52
  0.7 1.6 %copy-start.9 = (f32[4,128]{1,0:T(4,128)S(1)}, f32[4,128]{1,0:T(4,128)}, u32[]{:S(2)}) copy-start(f32[4,128]{1,0:T(4,128)} %param.6) | copy-start | bytes 6148
  40.0 0.7 copy-start.3
  56.6 32.5 %collective-permute-start = (f32[6,128,128]{2,1,0:T(8,128)}, f32[6,128,128]{2,1,0:T(8,128)S(1)}, u32[]{:S(2)}, u32[]{:S(2)}) collective-permute-start(f32[6,128,128]{2,1,0:T(8,128)} %constant_dynamic-slice_fusion), channel_id=1, source_target_pairs={{0,1},{1,0},{2,3},{3,2},{4,5},{5,4},{6,7},{7,6},{8,9},{9,8},{10,11... | collective-permute-start | bytes 1179656 | tf_op jit(solution)/shard_map/ppermute | solution.py:430
  57.9 0.9 copy-start
  58.8 29.4 %copy-start.1 = (f32[384,128]{1,0:T(8,128)S(1)}, f32[384,128]{1,0:T(8,128)}, u32[]{:S(2)}) copy-start(f32[384,128]{1,0:T(8,128)} %sum_first.1.gram_ref) | copy-start | bytes 589828
  71.4 0.7 copy-start.4
  72.0 0.7 copy-start.5
  89.1 0.9 copy-start.2
  90.0 0.9 copy-start.6

commit v2 on v1

--- a/solution.py
+++ b/solution.py
@@ -11,6 +11,7 @@
 MESH = pl.DeviceIdType.MESH
 HIGHEST = lax.Precision.HIGHEST
 HALF = 128
+CHUNKS = 2
 
 
 def dot(a, b, dims, precision=HIGHEST):
@@ -204,11 +205,15 @@
     lanes = lax.broadcasted_iota(jnp.int32, (8, width), 1)
     wide = lax.broadcasted_iota(jnp.int32, (count, width), 1)
 
-    def row_copy(source, step, a):
-        index = 2 * step + (0 if a < 0 else 1)
+    length = count // CHUNKS
+
+    def row_copy(source, step, a, c):
+        index = CHUNKS * (2 * step + (0 if a < 0 else 1)) + c
         target = below if a < 0 else above
+        span = pl.ds(c * length, length)
         return pltpu.make_async_remote_copy(
-            src_ref=source.at[0 if a < 0 else extent - 1], dst_ref=target.at[step],
+            src_ref=source.at[0 if a < 0 else extent - 1, :, span],
+            dst_ref=target.at[step, :, span],
             send_sem=send_row.at[index], recv_sem=recv_row.at[index],
             device_id=at(a, 0), device_id_type=MESH)
 
@@ -219,11 +224,19 @@
             send_sem=send_col.at[index], recv_sem=recv_col.at[index],
             device_id=at(a, b), device_id_type=MESH)
 
-    def exchange(source, step):
+    def start_rows(source, step, c):
         for a in (-1, 1):
             @pl.when(exists(a, 0))
             def _():
-                row_copy(source, step, a).start()
+                row_copy(source, step, a, c).start()
+
+    def wait_rows(source, step, c):
+        for a in (-1, 1):
+            @pl.when(exists(-a, 0))
+            def _():
+                row_copy(source, step, a, c).wait_recv()
+
+    def exchange_edges(source, step):
         for b in (-1, 1):
             packed = jnp.zeros((count, width), jnp.float32)
             for p in range(blocks):
@@ -246,12 +259,8 @@
             upper = arrived[index + corners.index((1, b))][blocks - comps : blocks]
             under = arrived[index + corners.index((-1, b))][:comps]
             halo[0 if b > 0 else 1] = jnp.concatenate([upper, centre, under, pad], axis=0).T
-        for a in (-1, 1):
-            @pl.when(exists(-a, 0))
-            def _():
-                row_copy(source, step, a).wait_recv()
-
-    def apply(source, step, store):
+
+    def apply(source, step, store, chunk):
         def tile(k, carry):
             at_k = pl.ds(pl.multiple_of(k * 8, 8), 8)
             acc = [[source[x, i, at_k] for x in range(extent)] for i in range(comps)]
@@ -279,7 +288,7 @@
                     store(x, i, k, modulus_ref[x : x + 1, :] * acc[i][x])
             return carry
 
-        lax.fori_loop(0, count // 8, tile, 0)
+        lax.fori_loop(chunk * length // 8, (chunk + 1) * length // 8, tile, 0)
 
     def store_once(x, i, k, value):
         once[x, i, pl.ds(pl.multiple_of(k * 8, 8), 8)] = value
@@ -288,36 +297,43 @@
         start = pl.multiple_of(mine * count + k * 8, 8)
         matrix_ref[comps * x + i, pl.ds(start, 8)] = value
 
-    exchange(field_ref, 0)
-    apply(field_ref, 0, store_once)
-    exchange(once, 1)
-    apply(once, 1, store_last)
-
     share = blocks // cols
 
-    def skc_copy(owner, to, part, o):
-        place = matrix_ref.at[pl.ds(part * share, share), pl.ds(pl.multiple_of(owner * count, 8), count)]
+    def skc_copy(owner, to, part, o, c):
+        start = pl.multiple_of(owner * count + c * length, 8)
+        place = matrix_ref.at[pl.ds(part * share, share), pl.ds(start, length)]
+        index = CHUNKS * (o - 1) + c
         return pltpu.make_async_remote_copy(
-            src_ref=place, dst_ref=place, send_sem=send_skc.at[o], recv_sem=recv_skc.at[o],
-            device_id={"skc": to}, device_id_type=MESH)
-
-    pairs = [(0, o) for o in range(1, cols)]
-    for n, (q, o) in enumerate(pairs):
-        to = skc_peer(o)
-        skc_copy(mine, to, lax.rem(to + q, cols), n).start()
-    for n, (q, o) in enumerate(pairs[: cols - 1]):
+            src_ref=place, dst_ref=place, send_sem=send_skc.at[index],
+            recv_sem=recv_skc.at[index], device_id={"skc": to}, device_id_type=MESH)
+
+    pairs = [(o, c) for c in range(CHUNKS) for o in range(1, cols)]
+    for c in range(CHUNKS):
+        start_rows(field_ref, 0, c)
+    exchange_edges(field_ref, 0)
+    for c in range(CHUNKS):
+        wait_rows(field_ref, 0, c)
+        apply(field_ref, 0, store_once, c)
+        start_rows(once, 1, c)
+    exchange_edges(once, 1)
+    for c in range(CHUNKS):
+        wait_rows(once, 1, c)
+        apply(once, 1, store_last, c)
+        for o in range(1, cols):
+            skc_copy(mine, skc_peer(o), skc_peer(o), o, c).start()
+    for o, c in pairs:
         owner = lax.rem(mine + cols - o, cols)
-        skc_copy(owner, owner, mine, n).wait_recv()
+        skc_copy(owner, owner, mine, o, c).wait_recv()
     part_ref[...] = pack_blocks(matrix_ref, mine * share, share)
-    for n, (q, o) in enumerate(pairs):
-        to = skc_peer(o)
-        skc_copy(mine, to, lax.rem(to + q, cols), n).wait_send()
+    for o, c in pairs:
+        skc_copy(mine, skc_peer(o), skc_peer(o), o, c).wait_send()
     for step in range(2):
         source = field_ref if step == 0 else once
         for a in (-1, 1):
             @pl.when(exists(a, 0))
             def _():
-                row_copy(source, step, a).wait_send()
+                for c in range(CHUNKS):
+                    row_copy(source, step, a, c).wait_send()
         for a, b in corners:
             @pl.when(exists(a, b))
             def _():
@@ -357,8 +373,8 @@
             pltpu.VMEM((4, edge_rows, count), f32),
             pltpu.VMEM((12, edge_rows, count), f32),
             pltpu.VMEM((2, count, width), f32),
-            dma((4,)), dma((4,)), dma((12,)), dma((12,)),
-            dma((cols - 1,)), dma((cols - 1,)),
+            dma((4 * CHUNKS,)), dma((4 * CHUNKS,)), dma((12,)), dma((12,)),
+            dma((CHUNKS * (cols - 1),)), dma((CHUNKS * (cols - 1),)),
         ],
         compiler_params=pltpu.CompilerParams(
             collective_id=3, has_side_effects=True, vmem_limit_bytes=40 * 1024 * 1024),

time: 104 us -> 101 us (0.971)
  Pallas kernels: 92.1 us -> 89.4 us
    pallas_call x1, Pallas kernels: 37.8 us -> 35.1 us  [sketch(): pl.pallas_call(functools.partial(sketch_kernel, cols, rows, planes), out_...]
where the time goes in v2:
time: 101 us
  Pallas kernels  89.4 us (89%)
  local copies, waits for them, and re-layouts  8.57 us (8%)
  starting transfers between devices  1.23 us (1%)
    pallas_call x1, Pallas kernels, sketch(): pl.pallas_call(functools.partial(sketch_kernel, cols, rows, planes), out_...  35.1 us
    pallas_call x2, Pallas kernels, reduce_all(): pl.pallas_call(functools.partial(reduce_kernel, planes, cols, rows), out_...  30.5 us
    pallas_call x1, Pallas kernels, body(): call(functools.partial(first_kernel, groups), [square, square, (share, to...  12.5 us
    pallas_call x1, Pallas kernels, body(): call(functools.partial(second_kernel, root_rows, groups), [(blocks, local...  11.2 us
    unnamed x24, local copies, waits for them, and re-layouts  6.18 us
  transfers between devices with their start and end apart: 1, of which 0 were waited for; matrix products, arithmetic and copies ran while one was open for 1% of the time, Pallas kernels for 27%

profile of v2, /device:TPU:0, one launch (start us, length us, event | category | flops | bytes accessed | tf_op | source)
XLA Modules:
  0.0 100.8 jit_solution(14740137374315024782)
XLA Ops:
  0.6 0.0 copy-start.8
  0.6 0.0 copy-start.7
  0.7 0.0 copy-start.10
  0.7 0.0 copy-start.9
  0.7 1.2 %copy.19 = f32[128,3,4,128]{3,0,1,2:T(8,128)S(1)} copy(f32[128,3,4,128]{3,2,1,0:T(4,128)} %param.5) | data formatting | bytes 1572864 | tf_op args[0]
  1.9 0.0 copy-done.8
  1.9 0.1 copy.13
  2.0 0.1 reshape.13.coupling_ref
  2.1 0.0 copy-done.7
  2.1 0.0 copy-done.10
  2.1 0.1 multiply_reduce_fusion
  2.2 0.0 copy-done.9
  2.2 35.1 %sketch.1 = (f32[12,256,128]{2,1,0:T(8,128)S(1)}, f32[384,128]{1,0:T(8,128)S(1)}) custom-call(f32[4,3,128,128]{3,2,1,0:T(8,128)S(1)} %bitcast.9, f32[4,128]{1,0:T(4,128)S(1)} %add.15.modulus_ref, f32[81]{0:T(128)S(1)} %reshape.13.coupling_ref), custom_call_target="tpu_custom_call" | custom-call | tf_op jit(solution)/shard_map/sketch/pallas_call | solution.py:361
  37.4 0.0 copy-start.3
  37.4 0.7 copy-done.3
  38.1 15.4 %sum_first.1.gram_ref = f32[384,128]{1,0:T(8,128)} custom-call(f32[384,128]{1,0:T(8,128)} %copy-done.3), custom_call_target="tpu_custom_call" | custom-call | tf_op jit(solution)/shard_map/sum_first/pallas_call | solution.py:88
  53.4 0.8 constant_dynamic-slice_fusion
  54.2 1.2 %collective-permute-start = (f32[6,128,128]{2,1,0:T(8,128)}, f32[6,128,128]{2,1,0:T(8,128)S(1)}, u32[]{:S(2)}, u32[]{:S(2)}) collective-permute-start(f32[6,128,128]{2,1,0:T(8,128)} %constant_dynamic-slice_fusion), channel_id=1, source_target_pairs={{0,1},{1,0},{2,3},{3,2},{4,5},{5,4},{6,7},{7,6},{8,9},{9,8},{10,11... | collective-permute-start | bytes 1179656 | tf_op jit(solution)/shard_map/ppermute | solution.py:446
  55.4 0.9 copy-done
  56.4 12.5 %first.1 = (f32[256,256]{1,0:T(8,128)S(1)}, f32[256,256]{1,0:T(8,128)S(1)}, f32[6,256,128]{2,1,0:T(8,128)S(1)}, f32[384,128]{1,0:T(8,128)S(1)}) custom-call(f32[384,128]{1,0:T(8,128)S(1)} %copy-done, f32[12,256,128]{2,1,0:T(8,128)S(1)} %get-tuple-element.20.matrix_ref), custom_call_target="tpu_custom_call" | custom-call | flops 5000000000 | bytes 40000000 | tf_op jit(solution)/shard_map/first/pallas_call | solution.py:463
  68.9 0.0 copy-start.4
  68.9 0.7 copy-done.4
  69.6 0.7 copy-done.5
  70.3 15.2 %sum_second.1.gram_ref = f32[384,128]{1,0:T(8,128)} custom-call(f32[384,128]{1,0:T(8,128)} %copy-done.4), custom_call_target="tpu_custom_call" | custom-call | tf_op jit(solution)/shard_map/sum_second/pallas_call | solution.py:88
  85.5 0.0 copy-done.1
  85.5 0.1 copy.15
  85.6 0.7 maximum_multiply_fusion
  86.3 0.0 collective-permute-done.refs_0_
  86.3 0.9 copy-done.2
  87.3 0.9 copy-done.6
  88.2 11.2 %second.1 = (f32[12,128,128]{2,1,0:T(8,128)S(1)}, f32[256,256]{1,0:T(8,128)}) custom-call(f32[384,128]{1,0:T(8,128)S(1)} %copy-done.2, f32[256,256]{1,0:T(8,128)S(1)} %get-tuple-element.17.upper_one_ref, f32[256,256]{1,0:T(8,128)S(1)} %copy-done.6, f32[6,256,128]{2,1,0:T(8,128)S(1)} %get-tuple-element.19.ortho_ref, ...), custom_call_target="tpu_custom_call" | custom-call | flops 5000000000 | bytes 40000000 | tf_op jit(solution)/shard_map/second/pallas_call | solution.py:468
  99.4 1.4 %copy.18 = f32[4,3,128,128]{3,0,1,2:T(4,128)} copy(f32[4,3,128,128]{3,2,1,0:T(8,128)S(1)} %bitcast.10) | data formatting | bytes 1572864 | tf_op jit(solution)/shard_map/reshape | solution.py:473
  (7 shorter events, 0.0 us)
Async XLA Ops:
  0.6 1.3 %copy-start.8 = (f32[9,3,3]{0,2,1:T(4,128)S(1)}, f32[9,3,3]{0,2,1:T(4,128)}, u32[]{:S(2)}) copy-start(f32[9,3,3]{0,2,1:T(4,128)} %param.9) | copy-start | bytes 976
  0.6 1.5 %copy-start.7 = (f32[4,4,128]{2,1,0:T(4,128)S(1)}, f32[4,4,128]{2,1,0:T(4,128)}, u32[]{:S(2)}) copy-start(f32[4,4,128]{2,1,0:T(4,128)} %param.7) | copy-start | bytes 24580
  0.7 1.5 %copy-start.10 = (f32[4]{0:T(128)S(1)}, f32[4]{0:T(128)}, u32[]{:S(2)}) copy-start(f32[4]{0:T(128)} %param.8) | copy-start | bytes 52
  0.7 1.6 %copy-start.9 = (f32[4,128]{1,0:T(4,128)S(1)}, f32[4,128]{1,0:T(4,128)}, u32[]{:S(2)}) copy-start(f32[4,128]{1,0:T(4,128)} %param.6) | copy-start | bytes 6148
  37.4 0.7 copy-start.3
  54.2 32.1 %collective-permute-start = (f32[6,128,128]{2,1,0:T(8,128)}, f32[6,128,128]{2,1,0:T(8,128)S(1)}, u32[]{:S(2)}, u32[]{:S(2)}) collective-permute-start(f32[6,128,128]{2,1,0:T(8,128)} %constant_dynamic-slice_fusion), channel_id=1, source_target_pairs={{0,1},{1,0},{2,3},{3,2},{4,5},{5,4},{6,7},{7,6},{8,9},{9,8},{10,11... | collective-permute-start | bytes 1179656 | tf_op jit(solution)/shard_map/ppermute | solution.py:446
  55.4 0.9 copy-start
  56.4 29.1 %copy-start.1 = (f32[384,128]{1,0:T(8,128)S(1)}, f32[384,128]{1,0:T(8,128)}, u32[]{:S(2)}) copy-start(f32[384,128]{1,0:T(8,128)} %sum_first.1.gram_ref) | copy-start | bytes 589828
  68.9 0.7 copy-start.4
  69.6 0.7 copy-start.5
  86.3 0.9 copy-start.2
  87.3 0.9 copy-start.6

commit v3 on v2

--- a/solution.py
+++ b/solution.py
@@ -11,7 +11,7 @@
 MESH = pl.DeviceIdType.MESH
 HIGHEST = lax.Precision.HIGHEST
 HALF = 128
-CHUNKS = 2
+CHUNKS = 4
 
 
 def dot(a, b, dims, precision=HIGHEST):

time: 101 us -> 100 us (0.990)
    pallas_call x1, Pallas kernels: 35.1 us -> 34 us  [sketch(): pl.pallas_call(functools.partial(sketch_kernel, cols, rows, planes), out_...]
  transfers between devices with their start and end apart: 1 -> 1, of which waited for: 0 -> 0; matrix products, arithmetic and copies ran while one was open for 1% -> 1% of each run, Pallas kernels for 27% -> 28%
where the time goes in v3:
time: 100 us; the launch traced here: 99.9 us
  Pallas kernels  88.4 us (88%)
  local copies, waits for them, and re-layouts  8.57 us (9%)
  starting transfers between devices  1.25 us (1%)
    pallas_call x1, Pallas kernels, sketch(): pl.pallas_call(functools.partial(sketch_kernel, cols, rows, planes), out_...  34 us
    pallas_call x2, Pallas kernels, reduce_all(): pl.pallas_call(functools.partial(reduce_kernel, planes, cols, rows), out_...  30.7 us
    pallas_call x1, Pallas kernels, body(): call(functools.partial(first_kernel, groups), [square, square, (share, to...  12.5 us
    pallas_call x1, Pallas kernels, body(): call(functools.partial(second_kernel, root_rows, groups), [(blocks, local...  11.2 us
    unnamed x24, local copies, waits for them, and re-layouts  6.18 us
  transfers between devices with their start and end apart: 1, of which 0 were waited for; matrix products, arithmetic and copies ran while one was open for 1% of the time, Pallas kernels for 28%

profile of v3, /device:TPU:0, one launch (start us, length us, event | category | flops | bytes accessed | tf_op | source)
XLA Modules:
  0.0 99.9 jit_solution(17578159182244052551)
XLA Ops:
  0.6 0.0 copy-start.8
  0.6 0.0 copy-start.7
  0.7 0.0 copy-start.10
  0.7 0.0 copy-start.9
  0.7 1.2 %copy.19 = f32[128,3,4,128]{3,0,1,2:T(8,128)S(1)} copy(f32[128,3,4,128]{3,2,1,0:T(4,128)} %param.5) | data formatting | bytes 1572864 | tf_op args[0]
  1.9 0.0 copy-done.8
  1.9 0.1 copy.13
  2.0 0.1 reshape.13.coupling_ref
  2.1 0.0 copy-done.7
  2.1 0.0 copy-done.10
  2.1 0.1 multiply_reduce_fusion
  2.2 0.0 copy-done.9
  2.2 34.0 %sketch.1 = (f32[12,256,128]{2,1,0:T(8,128)S(1)}, f32[384,128]{1,0:T(8,128)S(1)}) custom-call(f32[4,3,128,128]{3,2,1,0:T(8,128)S(1)} %bitcast.9, f32[4,128]{1,0:T(4,128)S(1)} %add.15.modulus_ref, f32[81]{0:T(128)S(1)} %reshape.13.coupling_ref), custom_call_target="tpu_custom_call" | custom-call | tf_op jit(solution)/shard_map/sketch/pallas_call | solution.py:361
  36.2 0.0 copy-start.3
  36.2 0.7 copy-done.3
  36.9 15.3 %sum_first.1.gram_ref = f32[384,128]{1,0:T(8,128)} custom-call(f32[384,128]{1,0:T(8,128)} %copy-done.3), custom_call_target="tpu_custom_call" | custom-call | tf_op jit(solution)/shard_map/sum_first/pallas_call | solution.py:88
  52.2 0.8 constant_dynamic-slice_fusion
  53.0 1.3 %collective-permute-start = (f32[6,128,128]{2,1,0:T(8,128)}, f32[6,128,128]{2,1,0:T(8,128)S(1)}, u32[]{:S(2)}, u32[]{:S(2)}) collective-permute-start(f32[6,128,128]{2,1,0:T(8,128)} %constant_dynamic-slice_fusion), channel_id=1, source_target_pairs={{0,1},{1,0},{2,3},{3,2},{4,5},{5,4},{6,7},{7,6},{8,9},{9,8},{10,11... | collective-permute-start | bytes 1179656 | tf_op jit(solution)/shard_map/ppermute | solution.py:446
  54.2 0.9 copy-done
  55.2 12.5 %first.1 = (f32[256,256]{1,0:T(8,128)S(1)}, f32[256,256]{1,0:T(8,128)S(1)}, f32[6,256,128]{2,1,0:T(8,128)S(1)}, f32[384,128]{1,0:T(8,128)S(1)}) custom-call(f32[384,128]{1,0:T(8,128)S(1)} %copy-done, f32[12,256,128]{2,1,0:T(8,128)S(1)} %get-tuple-element.20.matrix_ref), custom_call_target="tpu_custom_call" | custom-call | flops 5000000000 | bytes 40000000 | tf_op jit(solution)/shard_map/first/pallas_call | solution.py:463
  67.7 0.0 copy-start.4
  67.7 0.7 copy-done.4
  68.4 0.7 copy-done.5
  69.1 15.5 %sum_second.1.gram_ref = f32[384,128]{1,0:T(8,128)} custom-call(f32[384,128]{1,0:T(8,128)} %copy-done.4), custom_call_target="tpu_custom_call" | custom-call | tf_op jit(solution)/shard_map/sum_second/pallas_call | solution.py:88
  84.5 0.0 copy-done.1
  84.6 0.1 copy.15
  84.7 0.7 maximum_multiply_fusion
  85.4 0.0 collective-permute-done.refs_0_
  85.4 0.9 copy-done.2
  86.3 0.9 copy-done.6
  87.3 11.2 %second.1 = (f32[12,128,128]{2,1,0:T(8,128)S(1)}, f32[256,256]{1,0:T(8,128)}) custom-call(f32[384,128]{1,0:T(8,128)S(1)} %copy-done.2, f32[256,256]{1,0:T(8,128)S(1)} %get-tuple-element.17.upper_one_ref, f32[256,256]{1,0:T(8,128)S(1)} %copy-done.6, f32[6,256,128]{2,1,0:T(8,128)S(1)} %get-tuple-element.19.ortho_ref, ...), custom_call_target="tpu_custom_call" | custom-call | flops 5000000000 | bytes 40000000 | tf_op jit(solution)/shard_map/second/pallas_call | solution.py:468
  98.5 1.4 %copy.18 = f32[4,3,128,128]{3,0,1,2:T(4,128)} copy(f32[4,3,128,128]{3,2,1,0:T(8,128)S(1)} %bitcast.10) | data formatting | bytes 1572864 | tf_op jit(solution)/shard_map/reshape | solution.py:473
  (7 shorter events, 0.0 us)
Async XLA Ops:
  0.6 1.3 %copy-start.8 = (f32[9,3,3]{0,2,1:T(4,128)S(1)}, f32[9,3,3]{0,2,1:T(4,128)}, u32[]{:S(2)}) copy-start(f32[9,3,3]{0,2,1:T(4,128)} %param.9) | copy-start | bytes 976
  0.6 1.5 %copy-start.7 = (f32[4,4,128]{2,1,0:T(4,128)S(1)}, f32[4,4,128]{2,1,0:T(4,128)}, u32[]{:S(2)}) copy-start(f32[4,4,128]{2,1,0:T(4,128)} %param.7) | copy-start | bytes 24580
  0.7 1.5 %copy-start.10 = (f32[4]{0:T(128)S(1)}, f32[4]{0:T(128)}, u32[]{:S(2)}) copy-start(f32[4]{0:T(128)} %param.8) | copy-start | bytes 52
  0.7 1.6 %copy-start.9 = (f32[4,128]{1,0:T(4,128)S(1)}, f32[4,128]{1,0:T(4,128)}, u32[]{:S(2)}) copy-start(f32[4,128]{1,0:T(4,128)} %param.6) | copy-start | bytes 6148
  36.2 0.7 copy-start.3
  53.0 32.4 %collective-permute-start = (f32[6,128,128]{2,1,0:T(8,128)}, f32[6,128,128]{2,1,0:T(8,128)S(1)}, u32[]{:S(2)}, u32[]{:S(2)}) collective-permute-start(f32[6,128,128]{2,1,0:T(8,128)} %constant_dynamic-slice_fusion), channel_id=1, source_target_pairs={{0,1},{1,0},{2,3},{3,2},{4,5},{5,4},{6,7},{7,6},{8,9},{9,8},{10,11... | collective-permute-start | bytes 1179656 | tf_op jit(solution)/shard_map/ppermute | solution.py:446
  54.2 0.9 copy-start
  55.2 29.4 %copy-start.1 = (f32[384,128]{1,0:T(8,128)S(1)}, f32[384,128]{1,0:T(8,128)}, u32[]{:S(2)}) copy-start(f32[384,128]{1,0:T(8,128)} %sum_first.1.gram_ref) | copy-start | bytes 589828
  67.7 0.7 copy-start.4
  68.4 0.7 copy-start.5
  85.4 0.9 copy-start.2
  86.3 0.9 copy-start.6
